TPU v7x, 128 devices: a whole 4x4x4 slice. The times are simulated.
128 devices in a mesh: ia: 4 (over x_lo, core), ja: 16 (over z, y), ka: 2 (over x_hi).
Axes of the slice: x: 4 (x_hi: 2, x_lo: 2; x = x_hi * 2 + x_lo), y: 4, z: 4, core: 2. Of those that a mesh axis runs over, the one named last changes fastest.
Arguments:
- tensor: bfloat16 [1024, 2048, 512], P('ia', 'ja', 'ka'), may hold values from -6000 to 6000
- factor_b: float32 [2048, 256], P('ja'), may hold values from 0.1 to 1
- factor_c: float32 [512, 256], P('ka'), may hold values from 0.1 to 1
Outputs:
- factor_a: float32 [1024, 256], P('ia')
- refit_b: float32 [2048, 256], P('ja')
- refit_c: float32 [512, 256], P('ka')
All inputs are finite; a program needn't handle non-finite values.
Results may differ from a plain program's by a relative error of at most 0.009.
Values sent between devices are 32-bit elements; how exact they have to be, the bound alone decides.
No kernel may reach another device: no remote copies, remote signals or barrier semaphores. Data moves between devices by JAX's collectives and lax.ppermute only.
A program may use at most 128 MiB of HBM per device.

v0:
```python
import jax
import jax.numpy as jnp
from jax import lax
from jax.sharding import PartitionSpec as P

eps = 1e-06


def gram_of(matrix):
    return jnp.dot(
        matrix.T, matrix, precision=lax.Precision.HIGHEST, preferred_element_type=jnp.float32
    )


def solve_rows(moment, gram):
    lower = jnp.linalg.cholesky(gram)
    return jax.scipy.linalg.cho_solve((lower, True), moment.T).T


def local(tensor, factor_b, factor_c):
    rows_i, cols_j, deep_k = tensor.shape
    rank = factor_b.shape[1]
    total_i = rows_i * lax.axis_size("ia")
    total_j = cols_j * lax.axis_size("ja")
    total_k = deep_k * lax.axis_size("ka")
    gram_b = lax.psum(gram_of(factor_b), "ja")
    gram_c = lax.psum(gram_of(factor_c), "ka")
    flat = tensor.reshape(rows_i * cols_j, deep_k)
    inner = jnp.dot(flat, factor_c.astype(jnp.bfloat16), preferred_element_type=jnp.float32)
    inner = inner.reshape(rows_i, cols_j, rank)
    partial_a = jnp.sum(inner * factor_b[None, :, :], axis=1)
    mixed_a = gram_b * gram_c
    raw_a = solve_rows(lax.psum(partial_a, ("ja", "ka")), mixed_a)
    sums_a = lax.psum(jnp.sum(raw_a * raw_a, axis=0), "ia")
    factor_a = raw_a / jnp.sqrt(sums_a / total_i + eps)
    gram_a = lax.psum(gram_of(factor_a), "ia")
    partial_b = jnp.sum(inner * factor_a[:, None, :], axis=0)
    mixed_b = gram_a * gram_c
    raw_b = solve_rows(lax.psum(partial_b, ("ia", "ka")), mixed_b)
    sums_b = lax.psum(jnp.sum(raw_b * raw_b, axis=0), "ja")
    refit_b = raw_b / jnp.sqrt(sums_b / total_j + eps)
    gram_new_b = lax.psum(gram_of(refit_b), "ja")
    paired = (
        (factor_a[:, None, :] * refit_b[None, :, :])
        .reshape(rows_i * cols_j, rank)
        .astype(jnp.bfloat16)
    )
    partial_c = lax.dot_general(
        flat, paired, (((0,), (0,)), ((), ())), preferred_element_type=jnp.float32
    )
    mixed_c = gram_a * gram_new_b
    raw_c = solve_rows(lax.psum(partial_c, ("ia", "ja")), mixed_c)
    sums_c = lax.psum(jnp.sum(raw_c * raw_c, axis=0), "ka")
    refit_c = raw_c / jnp.sqrt(sums_c / total_k + eps)
    return (factor_a, refit_b, refit_c)


def solution(mesh):
    return jax.shard_map(
        local,
        mesh=mesh,
        in_specs=(P("ia", "ja", "ka"), P("ja", None), P("ka", None)),
        out_specs=(P("ia", None), P("ja", None), P("ka", None)),
        check_vma=False,
    )
```

profile of v0, /device:TPU:1, one launch (start us, length us, event | category | flops | bytes accessed | tf_op | source)
XLA Modules:
  0.0 1243.6 jit_solution(7279156568386695355)
XLA Ops:
  7.2 2.1 fusion.51
  9.4 2.3 fusion.52
  11.8 17.3 %multiply_reduce_fusion.1 = (f32[256,256]{1,0:T(8,128)}, f32[256,128,256]{2,1,0:T(8,128)}) fusion(f32[128,256]{1,0:T(8,128)} %param.7, bf16[256,128,256]{2,1,0:T(8,128)(2,1)} %param.6, f32[256,256]{1,0:T(8,128)} %param.8), kind=kOutput, calls=%fused_computation.8 | convolution fusion | flops 4311744512 | bytes 50987008 | tf_op jit(solution)/shard_map/dot_general | solution.py:29
  29.7 68.4 %all-reduce.9.cloned.1.call-done = f32[256,256]{0,1:T(8,128)} async-done(((f32[256,256]{0,1:T(8,128)}), f32[256,256]{0,1:T(8,128)}) %all-reduce.9.cloned.1.call-update) | async-done | bytes 262160 | tf_op jit(solution)/shard_map/psum | solution.py:26
  98.1 33.9 %all-reduce.11.cloned.1.call-done = f32[256,256]{0,1:T(8,128)} async-done(((f32[256,256]{0,1:T(8,128)}), f32[256,256]{0,1:T(8,128)}) %all-reduce.11.cloned.1.call-update) | async-done | bytes 262160 | tf_op jit(solution)/shard_map/psum | solution.py:27
  133.4 11.7 cholesky.172
  145.2 9.8 custom-call.24
  155.5 11.7 cholesky.189
  169.4 4.3 while.6
  170.2 1.4 bitcast_dynamic-update-slice_fusion.7
  172.3 1.4 bitcast_dynamic-update-slice_fusion.7
  173.7 19.7 %custom-call.25 = f32[2,128,128]{1,2,0:T(8,128)S(1)} custom-call(f32[2,128,128]{2,1,0:T(8,128)S(1)} %get-tuple-element.27), custom_call_target="InvertDiagBlocksLowerTriangular" | custom-call | tf_op jit(solution)/shard_map/jit(_cho_solve)/triangular_solve | solution.py:17
  193.4 268.7 %all-reduce.13.cloned.1.call-done = f32[256,256]{0,1:T(8,128)} async-done(((f32[256,256]{0,1:T(8,128)}), f32[256,256]{0,1:T(8,128)}) %all-reduce.13.cloned.1.call-update) | async-done | bytes 262160 | tf_op jit(solution)/shard_map/psum | solution.py:33
  465.9 26.9 %psum.73 = f32[256]{0:T(256)S(1)} all-reduce(f32[256]{0:T(256)S(1)} %multiply_reduce_fusion.3), channel_id=1, replica_groups=mesh['ia'=4,'ja'=16,'ka'=2] {'ia'}, use_global_device_ids=true, to_apply=%region_9.12 | all-reduce | flops 256 | bytes 2048 | tf_op jit(solution)/shard_map/psum | solution.py:34
  494.3 13.3 %multiply_reduce_fusion = f32[128,256]{1,0:T(8,128)} fusion(f32[256,128,256]{2,1,0:T(8,128)} %get-tuple-element.75, f32[256,256]{1,0:T(8,128)S(1)} %copy.16), kind=kLoop, calls=%fused_computation.7 | loop fusion | flops 16744448 | bytes 33947648 | tf_op jit(solution)/shard_map/reduce_sum | solution.py:37
  507.7 23.7 %all-reduce.15.cloned.1.call-done = f32[256,256]{0,1:T(8,128)} async-done(((f32[256,256]{0,1:T(8,128)}), f32[256,256]{0,1:T(8,128)}) %all-reduce.15.cloned.1.call-update) | async-done | bytes 262160 | tf_op jit(solution)/shard_map/psum | solution.py:36
  532.6 11.7 cholesky.206
  544.4 9.8 custom-call.26
  554.7 11.7 cholesky.223
  569.1 4.2 while.5
  570.0 1.4 bitcast_dynamic-update-slice_fusion.6
  573.3 19.7 %custom-call.20 = f32[2,128,128]{1,2,0:T(8,128)S(1)} custom-call(f32[2,128,128]{2,1,0:T(8,128)S(1)} %get-tuple-element.20), custom_call_target="InvertDiagBlocksLowerTriangular" | custom-call | tf_op jit(solution)/shard_map/jit(_cho_solve)/triangular_solve | solution.py:17
  596.4 33.8 %psum.76 = f32[256]{0:T(256)S(1)} all-reduce(f32[256]{0:T(256)S(1)} %multiply_reduce_fusion.4), channel_id=1, replica_groups=mesh['ia'=4,'ja'=16,'ka'=2] {'ja'}, use_global_device_ids=true, to_apply=%region_14.17 | all-reduce | flops 256 | bytes 2048 | tf_op jit(solution)/shard_map/psum | solution.py:40
  631.7 9.1 fusion.3
  640.8 76.3 %all-reduce.19.cloned.1.call-done = f32[256,256]{0,1:T(8,128)} async-done(((f32[256,256]{0,1:T(8,128)}), f32[256,256]{0,1:T(8,128)}) %all-reduce.19.cloned.1.call-update) | async-done | bytes 262160 | tf_op jit(solution)/shard_map/psum | solution.py:42
  718.3 11.7 cholesky.240
  730.1 9.8 custom-call.27
  740.4 11.7 cholesky.257
  754.8 4.0 while.7
  758.9 20.0 %custom-call.28 = f32[2,128,128]{1,2,0:T(8,128)S(1)} custom-call(f32[2,128,128]{2,1,0:T(8,128)S(1)} %get-tuple-element.28), custom_call_target="InvertDiagBlocksLowerTriangular" | custom-call | tf_op jit(solution)/shard_map/jit(_cho_solve)/triangular_solve | solution.py:17
  778.8 447.4 %all-reduce.21.cloned.1.call-done = f32[256,256]{1,0:T(8,128)} async-done(((f32[256,256]{1,0:T(8,128)}), f32[256,256]{1,0:T(8,128)}) %all-reduce.21.cloned.1.call-update) | async-done | bytes 262160 | tf_op jit(solution)/shard_map/psum | solution.py:52
  1230.0 5.3 psum.79
  (110 shorter events, 32.2 us)
Async XLA Ops:
  7.2 91.0 %all-reduce.9.cloned.1.call-start = ((), (), s32[]{:S(2)}) async-start(), calls=%async_computation | async-start | bytes 524288 | tf_op jit(solution)/shard_map/psum | solution.py:26
  9.3 122.7 %all-reduce.11.cloned.1.call-start = ((), (), s32[]{:S(2)}) async-start(), calls=%async_computation.1 | async-start | bytes 524288 | tf_op jit(solution)/shard_map/psum | solution.py:27
  11.7 450.3 %all-reduce.13.cloned.1.call-start = ((), (), s32[]{:S(2)}) async-start(), calls=%async_computation.2 | async-start | bytes 524288 | tf_op jit(solution)/shard_map/psum | solution.py:33
  29.1 502.2 %all-reduce.15.cloned.1.call-start = ((), (), s32[]{:S(2)}) async-start(), calls=%async_computation.3 | async-start | bytes 524288 | tf_op jit(solution)/shard_map/psum | solution.py:36
  132.1 399.3 %copy-start.1 = (f32[256,256]{0,1:T(8,128)S(1)}, f32[256,256]{0,1:T(8,128)}, u32[]{:S(2)}) copy-start(f32[256,256]{0,1:T(8,128)} %all-reduce.11.cloned.1.call-done) | copy-start | bytes 786436
  494.2 146.5 %copy-start = (f32[256,256]{1,0:T(8,128)}, f32[256,256]{1,0:T(8,128)S(1)}, u32[]{:S(2)}) copy-start(f32[256,256]{1,0:T(8,128)S(1)} %copy.16) | copy-start | bytes 786436
  494.3 98.8 %all-reduce.17.cloned.1.call-start = ((), (), s32[]{:S(2)}) async-start(), calls=%async_computation.4 | async-start | bytes 262144 | tf_op jit(solution)/shard_map/psum | solution.py:39
  507.7 209.5 %all-reduce.19.cloned.1.call-start = ((), (), s32[]{:S(2)}) async-start(), calls=%async_computation.5 | async-start | bytes 524288 | tf_op jit(solution)/shard_map/psum | solution.py:42
  531.4 185.8 %copy-start.2 = (f32[256,256]{0,1:T(8,128)S(1)}, f32[256,256]{0,1:T(8,128)}, u32[]{:S(2)}) copy-start(f32[256,256]{0,1:T(8,128)} %all-reduce.15.cloned.1.call-done) | copy-start | bytes 786436
  631.6 604.6 %copy-start.3 = (f32[128,256]{1,0:T(8,128)}, f32[128,256]{1,0:T(8,128)S(1)}, u32[]{:S(2)}) copy-start(f32[128,256]{1,0:T(8,128)S(1)} %copy.17) | copy-start | bytes 393220
  631.6 594.6 %all-reduce.21.cloned.1.call-start = ((), (), s32[]{:S(2)}) async-start(), calls=%async_computation.6 | async-start | bytes 524288 | tf_op jit(solution)/shard_map/psum | solution.py:52
Sparse Core Ops, SparseCore 0:
  11.7 86.3 all-reduce.8
  100.7 31.3 all-reduce.10
  135.1 326.8 all-reduce.12
  494.4 36.9 all-reduce.14
  534.1 58.1 all-reduce.16
  631.8 85.3 all-reduce.18
  720.2 506.0 all-reduce.20
where the time goes:
time: 1250 us; the launch traced here: 1240 us
  waiting for transfers between devices  919 us (74%)
  other arithmetic  180 us (14%)
  blocking collectives  66 us (5%)
  matrix products  45 us (4%)
  between operations  19 us (2%)
  local copies, waits for them, and re-layouts  13.6 us (1%)
    psum x1, waiting for transfers between devices, local(): raw_c = solve_rows(lax.psum(partial_c, ('ia', 'ja')), mixed_c)  447 us
    psum x1, waiting for transfers between devices, local(): raw_a = solve_rows(lax.psum(partial_a, ('ja', 'ka')), mixed_a)  269 us
    another operation x20, other arithmetic, solve_rows(): lower = jnp.linalg.cholesky(gram)  103 us
    psum x1, waiting for transfers between devices, local(): gram_new_b = lax.psum(gram_of(refit_b), 'ja')  76.3 us
    psum x1, waiting for transfers between devices, local(): gram_b = lax.psum(gram_of(factor_b), 'ja')  68.4 us
    another operation x7, other arithmetic, solve_rows(): return jax.scipy.linalg.cho_solve((lower, True), moment.T).T  59.4 us
    psum x1, waiting for transfers between devices, local(): gram_c = lax.psum(gram_of(factor_c), 'ka')  33.9 us
    psum x1, blocking collectives, local(): sums_b = lax.psum(jnp.sum(raw_b * raw_b, axis=0), 'ja')  33.8 us
  transfers between devices with their start and end apart: 7, of which 6 were waited for; matrix products, arithmetic and copies ran while one was open for 18% of the time, Pallas kernels for 0%

commit v1 on v0

v1 whole, which is shorter than its diff:
```python
import jax
import jax.numpy as jnp
from jax import lax
from jax.sharding import PartitionSpec as P

eps = 1e-06


def gram_of(matrix):
    return jnp.dot(
        matrix.T, matrix, precision=lax.Precision.HIGHEST, preferred_element_type=jnp.float32
    )


def solve_rows(moment, gram):
    lower = jnp.linalg.cholesky(gram)
    return jax.scipy.linalg.cho_solve((lower, True), moment.T).T


def scatter_sum(x, axes):
    n = lax.axis_size(axes)
    pieces = x.reshape(n, x.shape[0] // n, x.shape[1])
    return jnp.sum(lax.all_to_all(pieces, axes, 0, 0), axis=0)


def gather_rows(x, axes):
    n = lax.axis_size(axes)
    copies = jnp.broadcast_to(x[None], (n,) + x.shape)
    return lax.all_to_all(copies, axes, 0, 0).reshape(n * x.shape[0], x.shape[1])


def local(tensor, factor_b, factor_c):
    rows_i, cols_j, deep_k = tensor.shape
    rank = factor_b.shape[1]
    total_i = rows_i * lax.axis_size("ia")
    total_j = cols_j * lax.axis_size("ja")
    total_k = deep_k * lax.axis_size("ka")
    gram_b = gather_rows(scatter_sum(gram_of(factor_b), "ja"), "ja")
    own_c = gram_of(factor_c)
    gram_c = own_c + lax.ppermute(own_c, "ka", [(0, 1), (1, 0)])
    flat = tensor.reshape(rows_i * cols_j, deep_k)
    inner = jnp.dot(flat, factor_c.astype(jnp.bfloat16), preferred_element_type=jnp.float32)
    inner = inner.reshape(rows_i, cols_j, rank)
    partial_a = jnp.sum(inner * factor_b[None, :, :], axis=1)
    moment_a = gather_rows(scatter_sum(partial_a, ("ja", "ka")), ("ja", "ka"))
    raw_a = solve_rows(moment_a, gram_b * gram_c)
    raw_gram_a = gather_rows(scatter_sum(gram_of(raw_a), "ia"), "ia")
    scale_a = jnp.sqrt(jnp.diagonal(raw_gram_a) / total_i + eps)
    factor_a = raw_a / scale_a
    gram_a = raw_gram_a / scale_a[:, None] / scale_a[None, :]
    partial_b = jnp.sum(inner * factor_a[:, None, :], axis=0)
    moment_b = gather_rows(scatter_sum(partial_b, ("ia", "ka")), ("ia", "ka"))
    raw_b = solve_rows(moment_b, gram_a * gram_c)
    raw_gram_b = gather_rows(scatter_sum(gram_of(raw_b), "ja"), "ja")
    scale_b = jnp.sqrt(jnp.diagonal(raw_gram_b) / total_j + eps)
    refit_b = raw_b / scale_b
    gram_new_b = raw_gram_b / scale_b[:, None] / scale_b[None, :]
    paired = (
        (factor_a[:, None, :] * refit_b[None, :, :])
        .reshape(rows_i * cols_j, rank)
        .astype(jnp.bfloat16)
    )
    partial_c = lax.dot_general(
        flat, paired, (((0,), (0,)), ((), ())), preferred_element_type=jnp.float32
    )
    moment_c = gather_rows(scatter_sum(partial_c, ("ia", "ja")), ("ia", "ja", "ka"))
    raw_c = solve_rows(moment_c, gram_a * gram_new_b)
    scale_c = jnp.sqrt(jnp.sum(raw_c * raw_c, axis=0) / total_k + eps)
    mine = lax.axis_index("ka")
    share = deep_k // (lax.axis_size("ia") * lax.axis_size("ja"))
    spread = raw_c.reshape(-1, lax.axis_size("ka"), share, rank)
    raw_own = lax.dynamic_index_in_dim(spread, mine, 1, keepdims=False).reshape(deep_k, rank)
    refit_c = raw_own / scale_c
    return (factor_a, refit_b, refit_c)


def solution(mesh):
    return jax.shard_map(
        local,
        mesh=mesh,
        in_specs=(P("ia", "ja", "ka"), P("ja", None), P("ka", None)),
        out_specs=(P("ia", None), P("ja", None), P("ka", None)),
        check_vma=False,
    )
```

time: 1250 us -> 369 us (0.30)
  waiting for transfers between devices: 919 us -> 26.5 us
  starting transfers between devices: 0.81 us -> 63.5 us
  blocking collectives: 66 us -> 27.6 us
  between operations: 19 us -> 5.54 us
    psum x7 -> x0, waiting for transfers between devices: 919 us -> none  [the longest x1 447 us: local(): raw_c = solve_rows(lax.psum(partial_c, ('ia', 'ja')), mixed_c)]
    psum x3 -> x0, blocking collectives: 66 us -> none  [the longest x1 33.8 us: local(): sums_b = lax.psum(jnp.sum(raw_b * raw_b, axis=0), 'ja')]
    all_to_all x0 -> x10, starting transfers between devices: none -> 60.6 us  [the longest x4 30.7 us: scatter_sum(): return jnp.sum(lax.all_to_all(pieces, axes, 0, 0), axis=0)]
    all_to_all x0 -> x2, blocking collectives: none -> 27.6 us  [scatter_sum(): return jnp.sum(lax.all_to_all(pieces, axes, 0, 0), axis=0)]
    all_to_all x0 -> x10, waiting for transfers between devices: none -> 26.5 us  [the longest x6 20.1 us: gather_rows(): lax.all_to_all(copies, axes, 0, 0).reshape(n * x.shape[0], x.shape[1])]
  transfers between devices with their start and end apart: 7 -> 11, of which waited for: 6 -> 4; matrix products, arithmetic and copies ran while one was open for 18% -> 54% of each run, Pallas kernels for 0% -> 0%
where the time goes in v1:
time: 369 us; the launch traced here: 364 us
  other arithmetic  178 us (48%)
  starting transfers between devices  63.5 us (17%)
  matrix products  39 us (11%)
  blocking collectives  27.6 us (7%)
  waiting for transfers between devices  26.5 us (7%)
  local copies, waits for them, and re-layouts  24.1 us (7%)
  between operations  5.54 us (2%)
    another operation x20, other arithmetic, solve_rows(): lower = jnp.linalg.cholesky(gram)  103 us
    another operation x7, other arithmetic, solve_rows(): return jax.scipy.linalg.cho_solve((lower, True), moment.T).T  59.5 us
    all_to_all x4, starting transfers between devices, scatter_sum(): return jnp.sum(lax.all_to_all(pieces, axes, 0, 0), axis=0)  30.7 us
    all_to_all x6, starting transfers between devices, gather_rows(): lax.all_to_all(copies, axes, 0, 0).reshape(n * x.shape[0], x.shape[1])  30 us
    all_to_all x2, blocking collectives, scatter_sum(): return jnp.sum(lax.all_to_all(pieces, axes, 0, 0), axis=0)  27.6 us
    all_to_all x6, waiting for transfers between devices, gather_rows(): lax.all_to_all(copies, axes, 0, 0).reshape(n * x.shape[0], x.shape[1])  20.1 us
    dot_general x1, matrix products, local(): jnp.dot(flat, factor_c.astype(jnp.bfloat16), preferred_element_type=jnp.f...  17.3 us
    reduce_sum x1, other arithmetic, local(): partial_b = jnp.sum(inner * factor_a[:, None, :], axis=0)  13.3 us
  transfers between devices with their start and end apart: 11, of which 4 were waited for; matrix products, arithmetic and copies ran while one was open for 54% of the time, Pallas kernels for 0%

profile of v1, /device:TPU:1, one launch (start us, length us, event | category | flops | bytes accessed | tf_op | source)
XLA Modules:
  0.0 364.1 jit_solution(10157603923197518248)
XLA Ops:
  2.7 8.6 %all-to-all-start = ((f32[16,16,256]{2,1,0:T(8,128)}), f32[16,16,256]{2,1,0:T(8,128)S(1)}, u32[]{:S(2)}, u32[]{:S(2)}) async-start(f32[16,16,256]{2,1,0:T(8,128)} %bitcast), calls=%async_computation | async-start | bytes 524288 | tf_op jit(solution)/shard_map/all_to_all | solution.py:23
  11.3 17.3 %multiply_reduce_fusion.1 = (f32[256,256]{1,0:T(8,128)}, f32[256,128,256]{2,1,0:T(8,128)}) fusion(f32[128,256]{1,0:T(8,128)} %param.5, bf16[256,128,256]{2,1,0:T(8,128)(2,1)} %param.4, f32[256,256]{1,0:T(8,128)} %param.6), kind=kOutput, calls=%fused_computation.10 | convolution fusion | flops 4311744512 | bytes 50987008 | tf_op jit(solution)/shard_map/dot_general | solution.py:42
  28.6 9.4 %all-to-all-start.2 = ((f32[32,8,256]{2,1,0:T(8,128)}), f32[32,8,256]{2,1,0:T(8,128)S(1)}, u32[]{:S(2)}, u32[]{:S(2)}) async-start(f32[32,8,256]{2,1,0:T(8,128)} %bitcast.7), calls=%async_computation.2 | async-start | bytes 524288 | tf_op jit(solution)/shard_map/all_to_all | solution.py:23
  41.5 6.3 %all-to-all-done.2 = f32[32,8,256]{2,1,0:T(8,128)S(1)} async-done(((f32[32,8,256]{2,1,0:T(8,128)}), f32[32,8,256]{2,1,0:T(8,128)S(1)}, u32[]{:S(2)}, u32[]{:S(2)}) %all-to-all-start.2) | async-done | bytes 262176 | tf_op jit(solution)/shard_map/all_to_all | solution.py:23
  52.1 7.4 %all-to-all-done.1 = f32[16,16,256]{2,1,0:T(8,128)S(1)} async-done(((f32[16,16,256]{2,1,0:T(8,128)}), f32[16,16,256]{2,1,0:T(8,128)S(1)}, u32[]{:S(2)}, u32[]{:S(2)}) %all-to-all-start.1) | async-done | bytes 262176 | tf_op jit(solution)/shard_map/all_to_all | solution.py:29
  60.3 4.0 %all-to-all-start.3 = ((f32[32,8,256]{2,1,0:T(8,128)}), f32[32,8,256]{2,1,0:T(8,128)S(1)}, u32[]{:S(2)}, u32[]{:S(2)}) async-start(f32[32,8,256]{2,1,0:T(8,128)} %broadcast_in_dim.20), calls=%async_computation.3 | async-start | bytes 524288 | tf_op jit(solution)/shard_map/all_to_all | solution.py:29
  64.7 11.7 %cholesky.172 = f32[128,128]{1,0:T(8,128)S(1)} custom-call(f32[128,128]{1,0:T(8,128)S(1)} %cholesky.270), custom_call_target="Cholesky" | custom-call | tf_op jit(solution)/shard_map/jit(cholesky)/cholesky | solution.py:16
  76.5 9.8 %custom-call.38 = f32[1,128,128]{1,2,0:T(8,128)S(1)} custom-call(f32[1,128,128]{2,1,0:T(8,128)S(1)} %get-tuple-element.86), custom_call_target="InvertDiagBlocksLowerTriangular" | custom-call | tf_op jit(solution)/shard_map/jit(cholesky)/cholesky | solution.py:16
  86.8 11.7 %cholesky.189 = f32[128,128]{1,0:T(8,128)S(1)} custom-call(f32[128,128]{1,0:T(8,128)S(1)} %convolution_subtract_fusion.8), custom_call_target="Cholesky" | custom-call | tf_op jit(solution)/shard_map/jit(cholesky)/cholesky | solution.py:16
  100.6 3.9 %while.3 = (s32[]{:T(128)}, f32[256,256]{1,0:T(8,128)S(1)}, s32[2,2]{1,0:T(2,128)S(1)}, f32[2,128,128]{2,1,0:T(8,128)S(1)}, s32[]{:T(128)}) while((s32[]{:T(128)}, f32[256,256]{1,0:T(8,128)S(1)}, s32[2,2]{1,0:T(2,128)S(1)}, f32[2,128,128]{2,1,0:T(8,128)S(1)}, s32[]{:T(128)}) %tuple.70), condition=%wide.while_cond, body=%wide.while_body.sunk | while | flops 2 | bytes 131189 | solution.py:17
  104.6 20.1 %custom-call.29 = f32[2,128,128]{1,2,0:T(8,128)S(1)} custom-call(f32[2,128,128]{2,1,0:T(8,128)S(1)} %get-tuple-element.11), custom_call_target="InvertDiagBlocksLowerTriangular" | custom-call | tf_op jit(solution)/shard_map/jit(_cho_solve)/triangular_solve | solution.py:17
  127.4 12.7 %all_to_all.60 = f32[4,64,256]{2,1,0:T(8,128)S(1)} all-to-all(f32[4,64,256]{2,1,0:T(8,128)S(1)} %bitcast.157), channel_id=1, replica_groups=mesh['ia'=4,'ja'=16,'ka'=2] {'ia'}, dimensions={0} | all-to-all | bytes 524288 | tf_op jit(solution)/shard_map/all_to_all | solution.py:23
  140.8 4.4 %all-to-all-start.5 = ((f32[4,64,256]{2,1,0:T(8,128)}), f32[4,64,256]{2,1,0:T(8,128)S(1)}, u32[]{:S(2)}, u32[]{:S(2)}) async-start(f32[4,64,256]{2,1,0:T(8,128)} %broadcast_in_dim.21), calls=%async_computation.5 | async-start | bytes 524288 | tf_op jit(solution)/shard_map/all_to_all | solution.py:29
  145.2 5.2 %all-to-all-done.5 = f32[4,64,256]{2,1,0:T(8,128)S(1)} async-done(((f32[4,64,256]{2,1,0:T(8,128)}), f32[4,64,256]{2,1,0:T(8,128)S(1)}, u32[]{:S(2)}, u32[]{:S(2)}) %all-to-all-start.5) | async-done | bytes 262176 | tf_op jit(solution)/shard_map/all_to_all | solution.py:29
  153.0 13.3 %multiply_reduce_fusion = f32[128,256]{1,0:T(8,128)} fusion(f32[256,128,256]{2,1,0:T(8,128)} %get-tuple-element.90, f32[256,256]{1,0:T(8,128)S(1)} %get-tuple-element.88), kind=kLoop, calls=%fused_computation.9 | loop fusion | flops 16744448 | bytes 33947648 | tf_op jit(solution)/shard_map/reduce_sum | solution.py:51
  166.3 5.4 %all-to-all-start.6 = ((f32[8,16,256]{2,1,0:T(8,128)}), f32[8,16,256]{2,1,0:T(8,128)S(1)}, u32[]{:S(2)}, u32[]{:S(2)}) async-start(f32[8,16,256]{2,1,0:T(8,128)} %bitcast.19), calls=%async_computation.6 | async-start | bytes 262144 | tf_op jit(solution)/shard_map/all_to_all | solution.py:23
  172.0 11.7 %cholesky.206 = f32[128,128]{1,0:T(8,128)S(1)} custom-call(f32[128,128]{1,0:T(8,128)S(1)} %cholesky.273), custom_call_target="Cholesky" | custom-call | tf_op jit(solution)/shard_map/jit(cholesky)/cholesky | solution.py:16
  183.8 9.8 %custom-call.39 = f32[1,128,128]{1,2,0:T(8,128)S(1)} custom-call(f32[1,128,128]{2,1,0:T(8,128)S(1)} %get-tuple-element.82), custom_call_target="InvertDiagBlocksLowerTriangular" | custom-call | tf_op jit(solution)/shard_map/jit(cholesky)/cholesky | solution.py:16
  194.1 11.7 %cholesky.223 = f32[128,128]{1,0:T(8,128)S(1)} custom-call(f32[128,128]{1,0:T(8,128)S(1)} %convolution_subtract_fusion.7), custom_call_target="Cholesky" | custom-call | tf_op jit(solution)/shard_map/jit(cholesky)/cholesky | solution.py:16
  209.2 5.0 %all-to-all-start.7 = ((f32[8,16,256]{2,1,0:T(8,128)}), f32[8,16,256]{2,1,0:T(8,128)S(1)}, u32[]{:S(2)}, u32[]{:S(2)}) async-start(f32[8,16,256]{2,1,0:T(8,128)} %broadcast_in_dim.22), calls=%async_computation.7 | async-start | bytes 262144 | tf_op jit(solution)/shard_map/all_to_all | solution.py:29
  214.3 4.1 %while.4 = (s32[]{:T(128)}, f32[256,256]{1,0:T(8,128)S(1)}, s32[2,2]{1,0:T(2,128)S(1)}, f32[2,128,128]{2,1,0:T(8,128)S(1)}, s32[]{:T(128)}) while((s32[]{:T(128)}, f32[256,256]{1,0:T(8,128)S(1)}, s32[2,2]{1,0:T(2,128)S(1)}, f32[2,128,128]{2,1,0:T(8,128)S(1)}, s32[]{:T(128)}) %tuple.79), condition=%wide.while_cond.1, body=%wide.while_body.1.sunk | while | flops 2 | bytes 131189 | solution.py:17
  218.4 19.7 %custom-call.30 = f32[2,128,128]{1,2,0:T(8,128)S(1)} custom-call(f32[2,128,128]{2,1,0:T(8,128)S(1)} %get-tuple-element.19), custom_call_target="InvertDiagBlocksLowerTriangular" | custom-call | tf_op jit(solution)/shard_map/jit(_cho_solve)/triangular_solve | solution.py:17
  240.1 14.9 %all_to_all.61 = f32[16,16,256]{2,1,0:T(8,128)S(1)} all-to-all(f32[16,16,256]{2,1,0:T(8,128)S(1)} %bitcast.158), channel_id=1, replica_groups=mesh['ia'=4,'ja'=16,'ka'=2] {'ja'}, dimensions={0} | all-to-all | bytes 524288 | tf_op jit(solution)/shard_map/all_to_all | solution.py:23
  259.3 7.5 %all-to-all-done.9 = f32[16,16,256]{2,1,0:T(8,128)S(1)} async-done(((f32[16,16,256]{2,1,0:T(8,128)}), f32[16,16,256]{2,1,0:T(8,128)S(1)}, u32[]{:S(2)}, u32[]{:S(2)}) %all-to-all-start.9) | async-done | bytes 262176 | tf_op jit(solution)/shard_map/all_to_all | solution.py:29
  269.5 11.0 %fusion.3 = f32[256,256]{1,0:T(8,128)S(1)} fusion(bf16[256,128,256]{2,1,0:T(8,128)(2,1)} %param.4, f32[128,256]{1,0:T(8,128)S(1)} %copy.80, f32[256,256]{1,0:T(8,128)S(1)} %get-tuple-element.88), kind=kOutput, calls=%fused_computation.16 | convolution fusion | flops 4311744512 | bytes 17432576 | tf_op jit(solution)/shard_map/dot_general | solution.py:63
  281.3 7.2 %all-to-all-start.10 = ((f32[64,4,256]{2,1,0:T(4,128)}), f32[64,4,256]{2,1,0:T(4,128)S(1)}, u32[]{:S(2)}, u32[]{:S(2)}) async-start(f32[64,4,256]{2,1,0:T(4,128)} %reshape.148), calls=%async_computation.10 | async-start | bytes 524288 | tf_op jit(solution)/shard_map/all_to_all | solution.py:23
  288.9 11.7 %cholesky.240 = f32[128,128]{1,0:T(8,128)S(1)} custom-call(f32[128,128]{1,0:T(8,128)S(1)} %cholesky.276), custom_call_target="Cholesky" | custom-call | tf_op jit(solution)/shard_map/jit(cholesky)/cholesky | solution.py:16
  300.7 9.8 %custom-call.40 = f32[1,128,128]{1,2,0:T(8,128)S(1)} custom-call(f32[1,128,128]{2,1,0:T(8,128)S(1)} %get-tuple-element.78), custom_call_target="InvertDiagBlocksLowerTriangular" | custom-call | tf_op jit(solution)/shard_map/jit(cholesky)/cholesky | solution.py:16
  311.0 11.7 %cholesky.257 = f32[128,128]{1,0:T(8,128)S(1)} custom-call(f32[128,128]{1,0:T(8,128)S(1)} %convolution_subtract_fusion.4), custom_call_target="Cholesky" | custom-call | tf_op jit(solution)/shard_map/jit(cholesky)/cholesky | solution.py:16
  326.3 9.4 %all-to-all-start.11 = ((f32[128,4,256]{2,1,0:T(4,128)}), f32[128,4,256]{2,1,0:T(4,128)S(1)}, u32[]{:S(2)}, u32[]{:S(2)}) async-start(f32[128,4,256]{2,1,0:T(4,128)} %broadcast_in_dim.24), calls=%async_computation.11 | async-start | bytes 1048576 | tf_op jit(solution)/shard_map/all_to_all | solution.py:29
  335.8 4.1 %while.5 = (s32[]{:T(128)}, f32[256,256]{1,0:T(8,128)S(1)}, s32[2,2]{1,0:T(2,128)S(1)}, f32[2,128,128]{2,1,0:T(8,128)S(1)}, s32[]{:T(128)}) while((s32[]{:T(128)}, f32[256,256]{1,0:T(8,128)S(1)}, s32[2,2]{1,0:T(2,128)S(1)}, f32[2,128,128]{2,1,0:T(8,128)S(1)}, s32[]{:T(128)}) %tuple.80), condition=%wide.while_cond.2, body=%wide.while_body.2.sunk | while | flops 2 | bytes 131189 | solution.py:17
  339.9 19.7 %custom-call.31 = f32[2,128,128]{1,2,0:T(8,128)S(1)} custom-call(f32[2,128,128]{2,1,0:T(8,128)S(1)} %get-tuple-element.27), custom_call_target="InvertDiagBlocksLowerTriangular" | custom-call | tf_op jit(solution)/shard_map/jit(_cho_solve)/triangular_solve | solution.py:17
  (132 shorter events, 50.1 us)
Async XLA Ops:
  2.7 25.9 %all-to-all-start = ((f32[16,16,256]{2,1,0:T(8,128)}), f32[16,16,256]{2,1,0:T(8,128)S(1)}, u32[]{:S(2)}, u32[]{:S(2)}) async-start(f32[16,16,256]{2,1,0:T(8,128)} %bitcast), calls=%async_computation | async-start | bytes 524288 | tf_op jit(solution)/shard_map/all_to_all | solution.py:23
  11.3 26.7 %copy-start = (f32[256,256]{1,0:T(8,128)S(1)}, f32[256,256]{1,0:T(8,128)}, u32[]{:S(2)}) copy-start(f32[256,256]{1,0:T(8,128)} %param.6) | copy-start | bytes 786436
  28.6 19.2 %all-to-all-start.2 = ((f32[32,8,256]{2,1,0:T(8,128)}), f32[32,8,256]{2,1,0:T(8,128)S(1)}, u32[]{:S(2)}, u32[]{:S(2)}) async-start(f32[32,8,256]{2,1,0:T(8,128)} %bitcast.7), calls=%async_computation.2 | async-start | bytes 524288 | tf_op jit(solution)/shard_map/all_to_all | solution.py:23
  38.6 25.9 %collective-permute-start = (f32[256,256]{0,1:T(8,128)S(1)}, f32[256,256]{0,1:T(8,128)S(1)}, u32[]{:S(2)}, u32[]{:S(2)}) collective-permute-start(f32[256,256]{0,1:T(8,128)S(1)} %fusion.50), channel_id=1, source_target_pairs={{0,1},{1,0},{2,3},{3,2},{4,5},{5,4},{6,7},{7,6},{8,9},{9,8},{10,11... | collective-permute-start | bytes 786440 | tf_op jit(solution)/shard_map/ppermute | solution.py:40
  48.5 11.0 %all-to-all-start.1 = ((f32[16,16,256]{2,1,0:T(8,128)}), f32[16,16,256]{2,1,0:T(8,128)S(1)}, u32[]{:S(2)}, u32[]{:S(2)}) async-start(f32[16,16,256]{2,1,0:T(8,128)} %broadcast_in_dim.19), calls=%async_computation.1 | async-start | bytes 524288 | tf_op jit(solution)/shard_map/all_to_all | solution.py:29
  60.3 64.4 %all-to-all-start.3 = ((f32[32,8,256]{2,1,0:T(8,128)}), f32[32,8,256]{2,1,0:T(8,128)S(1)}, u32[]{:S(2)}, u32[]{:S(2)}) async-start(f32[32,8,256]{2,1,0:T(8,128)} %broadcast_in_dim.20), calls=%async_computation.3 | async-start | bytes 524288 | tf_op jit(solution)/shard_map/all_to_all | solution.py:29
  140.8 9.6 %all-to-all-start.5 = ((f32[4,64,256]{2,1,0:T(8,128)}), f32[4,64,256]{2,1,0:T(8,128)S(1)}, u32[]{:S(2)}, u32[]{:S(2)}) async-start(f32[4,64,256]{2,1,0:T(8,128)} %broadcast_in_dim.21), calls=%async_computation.5 | async-start | bytes 524288 | tf_op jit(solution)/shard_map/all_to_all | solution.py:29
  153.0 127.5 %copy-start.1 = (f32[256,256]{1,0:T(8,128)}, f32[256,256]{1,0:T(8,128)S(1)}, u32[]{:S(2)}) copy-start(f32[256,256]{1,0:T(8,128)S(1)} %get-tuple-element.88) | copy-start | bytes 786436
  166.3 42.2 %all-to-all-start.6 = ((f32[8,16,256]{2,1,0:T(8,128)}), f32[8,16,256]{2,1,0:T(8,128)S(1)}, u32[]{:S(2)}, u32[]{:S(2)}) async-start(f32[8,16,256]{2,1,0:T(8,128)} %bitcast.19), calls=%async_computation.6 | async-start | bytes 262144 | tf_op jit(solution)/shard_map/all_to_all | solution.py:23
  209.2 28.8 %all-to-all-start.7 = ((f32[8,16,256]{2,1,0:T(8,128)}), f32[8,16,256]{2,1,0:T(8,128)S(1)}, u32[]{:S(2)}, u32[]{:S(2)}) async-start(f32[8,16,256]{2,1,0:T(8,128)} %broadcast_in_dim.22), calls=%async_computation.7 | async-start | bytes 262144 | tf_op jit(solution)/shard_map/all_to_all | solution.py:29
  255.8 11.0 %all-to-all-start.9 = ((f32[16,16,256]{2,1,0:T(8,128)}), f32[16,16,256]{2,1,0:T(8,128)S(1)}, u32[]{:S(2)}, u32[]{:S(2)}) async-start(f32[16,16,256]{2,1,0:T(8,128)} %broadcast_in_dim.23), calls=%async_computation.9 | async-start | bytes 524288 | tf_op jit(solution)/shard_map/all_to_all | solution.py:29
  269.5 94.3 %copy-start.2 = (f32[128,256]{1,0:T(8,128)}, f32[128,256]{1,0:T(8,128)S(1)}, u32[]{:S(2)}) copy-start(f32[128,256]{1,0:T(8,128)S(1)} %copy.80) | copy-start | bytes 393220
  281.3 44.1 %all-to-all-start.10 = ((f32[64,4,256]{2,1,0:T(4,128)}), f32[64,4,256]{2,1,0:T(4,128)S(1)}, u32[]{:S(2)}, u32[]{:S(2)}) async-start(f32[64,4,256]{2,1,0:T(4,128)} %reshape.148), calls=%async_computation.10 | async-start | bytes 524288 | tf_op jit(solution)/shard_map/all_to_all | solution.py:23
  326.3 33.3 %all-to-all-start.11 = ((f32[128,4,256]{2,1,0:T(4,128)}), f32[128,4,256]{2,1,0:T(4,128)S(1)}, u32[]{:S(2)}, u32[]{:S(2)}) async-start(f32[128,4,256]{2,1,0:T(4,128)} %broadcast_in_dim.24), calls=%async_computation.11 | async-start | bytes 1048576 | tf_op jit(solution)/shard_map/all_to_all | solution.py:29
